TPU v7x, 256 devices: a whole 4x4x8 slice. The times are simulated.
256 devices in a mesh: ctx: 64 (over z, y, core), head: 4 (over x).
Axes of the slice: x: 4, y: 4, z: 8, core: 2. Of those that a mesh axis runs over, the one named last changes fastest.
Arguments:
- queries: bfloat16 [8192, 36864], P('ctx', 'head'), may hold values from -25 to 25
- cache_latent: bfloat16 [262144, 576], P('ctx'), may hold values from -4 to 4
- cache_scales: float32 [262144, 5], P('ctx'), may hold values from 0.3 to 3
- index_keys: bfloat16 [262144, 128], P('ctx'), may hold values from -6 to 6
- index_queries: bfloat16 [8192, 8192], P('ctx', 'head'), may hold values from -6 to 6
- index_weights: bfloat16 [8192, 64], P('ctx', 'head'), may hold values from -0.75 to 0.75
- value_up: bfloat16 [64, 512, 128], P('head'), may hold values from -1 to 1
- selections: int32 [128, 32], P('ctx'), may hold values from 0 to 4095, as said below
Outputs:
- attn_out: bfloat16 [8192, 8192], P('ctx', 'head')
- index_logits: float32 [8192, 2048], P('ctx', 'head')
Inputs may be any that keep to these rules, and one draw needn't show every extreme that they name: `selections`: row r names 32 different blocks by global index, block b holding cache tokens b * 64 to b * 64 + 63 and lying on ctx index b // 64. No named block lies after d(r) = (r // 2) * 64 + 62 + r % 2, the block of row r's own query tokens, and d(r) is always named. Over the 2 rows of one ctx index, the named blocks that lie on any one other ctx index are at most 2 different ones; for ctx index 0 they are exactly 2, from every other ctx index.
All inputs are finite; a program needn't handle non-finite values.
Results may differ from a plain program's by a relative error of at most 0.014.
Values may be sent and summed in bfloat16 or wider, within the bound.
A program may use at most 128 MiB of HBM per device.

v0:
```python
from functools import partial

import jax
import jax.numpy as jnp
from jax import lax
from jax.sharding import PartitionSpec as P

D_LAT = 512
D_ROPE = 64
NOPE_DIM = 128
D_HEAD = 128
IDX_DIM = 128
BLOCK = 64
SEL = 32
CAP = 2
D_KEY = 576


def dequantize(cache_latent, cache_scales, index_keys):
    tok_count = cache_latent.shape[0]
    group_width = D_LAT // 4
    latent_nope = cache_latent[:, :D_LAT].astype(jnp.float32).reshape(tok_count, 4, group_width)
    latent_nope = (latent_nope * cache_scales[:, :4, None]).reshape(tok_count, D_LAT)
    latent_full = jnp.concatenate(
        [latent_nope, cache_latent[:, D_LAT:].astype(jnp.float32)], axis=1
    )
    idx_key = index_keys.astype(jnp.float32) * cache_scales[:, 4:5]
    return (latent_full.astype(jnp.bfloat16), idx_key.astype(jnp.bfloat16))


def visibility(chosen, diagonal):
    offsets = jnp.arange(BLOCK, dtype=jnp.int32)
    earlier = chosen < diagonal
    later_ok = offsets[None, :] <= offsets[:, None]
    visible = earlier[None, :, None] | later_ok[:, None, :]
    return visible.reshape(BLOCK, SEL * BLOCK)


def attend_block(block_items, value_up):
    query_rows, picked, visible = block_items
    score_scale = (NOPE_DIM + D_ROPE) ** (-0.5)
    scores = (
        jnp.einsum("bhd,kd->bhk", query_rows, picked, preferred_element_type=jnp.float32)
        * score_scale
    )
    masked = jnp.where(visible[:, None, :], scores, -1e30)
    top_score = jnp.max(masked, axis=2, keepdims=True)
    weights = jnp.where(visible[:, None, :], jnp.exp(masked - top_score), 0.0)
    prob_rows = (weights / jnp.sum(weights, axis=2, keepdims=True)).astype(jnp.bfloat16)
    attended = jnp.einsum(
        "bhk,kd->bhd", prob_rows, picked[:, :D_LAT], preferred_element_type=jnp.float32
    ).astype(jnp.bfloat16)
    head_out = jnp.einsum("bhd,hde->bhe", attended, value_up, preferred_element_type=jnp.float32)
    return head_out.astype(jnp.bfloat16).reshape(query_rows.shape[0], -1)


def index_block(block_items):
    iquery, iweight, picked_keys, visible = block_items
    idx_dots = jnp.einsum(
        "bgd,kd->bgk", iquery, picked_keys, preferred_element_type=jnp.float32
    ) * IDX_DIM ** (-0.5)
    logits = jnp.sum(iweight.astype(jnp.float32)[:, :, None] * jnp.maximum(idx_dots, 0.0), axis=1)
    return jnp.where(visible, logits, 0.0)


def local(
    queries,
    cache_latent,
    cache_scales,
    index_keys,
    index_queries,
    index_weights,
    value_up,
    selections,
):
    ctx_count = lax.axis_size("ctx")
    ctx_place = lax.axis_index("ctx")
    kblocks = cache_latent.shape[0] // BLOCK
    qblocks = selections.shape[0]
    latent, idx_key = dequantize(cache_latent, cache_scales, index_keys)
    latent_blocks = latent.reshape(kblocks, BLOCK, D_KEY)
    key_blocks = idx_key.reshape(kblocks, BLOCK, IDX_DIM)
    chosen = selections.reshape(-1)
    owners = chosen // kblocks
    local_ids = chosen % kblocks
    every_block = jnp.arange(ctx_count * kblocks, dtype=jnp.int32)
    wanted = jnp.any(chosen[:, None] == every_block[None, :], axis=0).reshape(ctx_count, kblocks)
    wanted = wanted & (jnp.arange(ctx_count, dtype=jnp.int32)[:, None] != ctx_place)
    slot_rank = jnp.cumsum(wanted.astype(jnp.int32), axis=1) - 1
    slot_hit = wanted[:, :, None] & (
        slot_rank[:, :, None] == jnp.arange(CAP, dtype=jnp.int32)[None, None, :]
    )
    block_ids = jnp.sum(
        jnp.where(slot_hit, jnp.arange(kblocks, dtype=jnp.int32)[None, :, None], 0), axis=1
    )
    requests = jnp.where(jnp.any(slot_hit, axis=1), block_ids, -1)
    asked_ids = jnp.maximum(
        lax.all_to_all(requests, "ctx", split_axis=0, concat_axis=0, tiled=True), 0
    )
    from_remote = jnp.clip(owners * CAP + slot_rank.reshape(-1)[chosen], 0, ctx_count * CAP - 1)
    is_local = (owners == ctx_place)[:, None, None]
    got_lat, got_key = (
        lax.all_to_all(latent_blocks[asked_ids], "ctx", split_axis=0, concat_axis=0, tiled=True),
        lax.all_to_all(key_blocks[asked_ids], "ctx", split_axis=0, concat_axis=0, tiled=True),
    )
    pick_lat = jnp.where(
        is_local,
        latent_blocks[local_ids],
        got_lat.reshape(ctx_count * CAP, BLOCK, D_KEY)[from_remote],
    )
    pick_key = jnp.where(
        is_local,
        key_blocks[local_ids],
        got_key.reshape(ctx_count * CAP, BLOCK, IDX_DIM)[from_remote],
    )
    picked = pick_lat.reshape(qblocks, SEL * BLOCK, D_KEY)
    picked_keys = pick_key.reshape(qblocks, SEL * BLOCK, IDX_DIM)
    diagonals = ctx_place * kblocks + kblocks - qblocks + jnp.arange(qblocks, dtype=jnp.int32)
    visible = jax.vmap(visibility)(selections, diagonals)
    heads_here = queries.shape[1] // D_KEY
    query_blocks = queries.reshape(qblocks, BLOCK, heads_here, D_KEY)
    attn_rows = lax.map(partial(attend_block, value_up=value_up), (query_blocks, picked, visible))
    attn_out = attn_rows.reshape(-1, heads_here * D_HEAD)
    idx_here = index_weights.shape[1]
    head_terms = lax.map(
        index_block,
        (
            index_queries.reshape(qblocks, BLOCK, idx_here, IDX_DIM),
            index_weights.reshape(qblocks, BLOCK, idx_here),
            picked_keys,
            visible,
        ),
    )
    index_logits = lax.psum_scatter(
        head_terms.reshape(-1, SEL * BLOCK).astype(jnp.bfloat16),
        "head",
        scatter_dimension=1,
        tiled=True,
    ).astype(jnp.float32)
    return (attn_out, index_logits)


def solution(mesh):
    return jax.shard_map(
        local,
        mesh=mesh,
        in_specs=(
            P("ctx", "head"),
            P("ctx", None),
            P("ctx", None),
            P("ctx", None),
            P("ctx", "head"),
            P("ctx", "head"),
            P("head", None, None),
            P("ctx", None),
        ),
        out_specs=(P("ctx", "head"), P("ctx", "head")),
        check_vma=False,
    )
```

profile of v0, /device:TPU:1, one launch (start us, length us, event | category | flops | bytes accessed | tf_op | source)
XLA Modules:
  0.0 413.4 jit_solution(7620468944037036188)
XLA Ops:
  9.5 13.2 %all-to-all-start = ((s32[64,1,2]{2,1,0:T(1,128)}), s32[64,1,2]{2,1,0:T(1,128)S(1)}, u32[]{:S(2)}, u32[]{:S(2)}) async-start(s32[64,1,2]{2,1,0:T(1,128)} %copy.34), calls=%async_computation | async-start | bytes 65536 | tf_op jit(solution)/shard_map/all_to_all | solution.py:98
  25.4 6.6 %all-to-all-done = s32[64,1,2]{2,1,0:T(1,128)S(1)} async-done(((s32[64,1,2]{2,1,0:T(1,128)}), s32[64,1,2]{2,1,0:T(1,128)S(1)}, u32[]{:S(2)}, u32[]{:S(2)}) %all-to-all-start) | async-done | bytes 544 | tf_op jit(solution)/shard_map/all_to_all | solution.py:98
  34.5 5.6 %all-to-all-start.2 = ((bf16[64,2,64,128]{3,2,1,0:T(8,128)(2,1)}), bf16[64,2,64,128]{3,2,1,0:T(8,128)(2,1)}, u32[]{:S(2)}, u32[]{:S(2)}) async-start(bf16[64,2,64,128]{3,2,1,0:T(8,128)(2,1)} %bitcast.27), calls=%async_computation.2 | async-start | bytes 4194304 | tf_op jit(solution)/shard_map/all_to_all | solution.py:104
  40.1 4.7 %slice.15 = bf16[4096,512]{0,1:T(8,128)(2,1)} slice(bf16[4096,576]{0,1:T(8,128)(2,1)} %param.13), slice={[0:4096], [0:512]} | slice | bytes 8388608 | tf_op jit(solution)/shard_map/slice | solution.py:22
  47.3 6.5 %copy.39 = bf16[4096,512]{1,0:T(8,128)(2,1)} copy(bf16[4096,512]{0,1:T(8,128)(2,1)} %slice.15) | data formatting | bytes 8388608
  56.1 9.4 %mul.52 = f32[4096,4,128]{2,1,0:T(4,128)S(1)} broadcast(f32[4096,4]{1,0:T(8,128)S(1)} %copy.32), dimensions={0,1} | broadcast | bytes 8454144 | tf_op jit(solution)/shard_map/mul | solution.py:23
  65.5 5.9 %fusion.33 = bf16[4096,512]{1,0:T(8,128)(2,1)} fusion(f32[512,8,4,128]{3,2,1,0:T(4,128)S(1)} %bitcast.106, bf16[4096,512]{1,0:T(8,128)(2,1)} %copy.39), kind=kLoop, calls=%fused_computation.43 | loop fusion | flops 6291456 | bytes 16777216 | tf_op jit(solution)/shard_map/convert.4
  71.5 5.3 %pad_maximum_fusion = bf16[64,64,576]{2,1,0:T(8,128)(2,1)} fusion(bf16[64,64,64]{2,1,0:T(8,128)(2,1)S(1)} %bitcast.114, bf16[64,64,512]{2,1,0:T(8,128)(2,1)} %bitcast.111), kind=kLoop, calls=%fused_computation.44 | loop fusion | flops 9437184 | bytes 9437184 | tf_op jit(solution)/shard_map/concatenate | solution.py:24
  76.8 10.2 %gather_fusion.1 = bf16[128,64,576]{2,1,0:T(8,128)(2,1)} fusion(bf16[64,64,576]{2,1,0:T(8,128)(2,1)} %pad_maximum_fusion, s32[1024]{0:T(1024)S(1)} %pad_clamp_fusion.2), kind=kCustom, calls=%fused_computation.1 | custom fusion | bytes 18874880 | tf_op jit(solution)/shard_map/gather | solution.py:103
  89.7 7.8 %all-to-all-start.1 = ((bf16[64,2,64,576]{3,2,1,0:T(8,128)(2,1)}), bf16[64,2,64,576]{3,2,1,0:T(8,128)(2,1)}, u32[]{:S(2)}, u32[]{:S(2)}) async-start(bf16[64,2,64,576]{3,2,1,0:T(8,128)(2,1)} %bitcast.105), calls=%async_computation.1 | async-start | bytes 20971520 | tf_op jit(solution)/shard_map/all_to_all | solution.py:103
  106.3 7.0 %while.21 = (s32[]{:T(128)}, bf16[2,64,2048]{2,1,0:T(8,128)(2,1)S(1)}, pred[2,64,2048]{2,1,0:T(8,128)(4,1)S(1)}, bf16[2,64,16]{2,1,0:T(8,128)(2,1)S(1)}, bf16[2,...) while((s32[]{:T(128)}, bf16[2,64,2048]{2,1,0:T(8,128)(2,1)S(1)}, ...), condition=%wide.region_10.11_spmd, body=%wide.region_8.10_spmd.sunk | while | flops 545260544 | bytes 1715285 | solution.py:125
  114.2 6.2 %gather_fusion = bf16[64,64,576]{2,1,0:T(8,128)(2,1)} fusion(bf16[64,64,576]{2,1,0:T(8,128)(2,1)} %pad_maximum_fusion, s32[1024]{0:T(1024)S(1)} %get-tuple-element.119), kind=kCustom, calls=%fused_computation | custom fusion | bytes 9437440 | tf_op jit(solution)/shard_map/gather | solution.py:108
  123.8 13.9 %reduce-scatter.2.cloned.1.call-done = bf16[128,512]{1,0:T(8,128)(2,1)} async-done(((bf16[128,2048]{1,0:T(8,128)(2,1)}), bf16[128,512]{1,0:T(8,128)(2,1)}) %reduce-scatter.2.cloned.1.call-update) | async-done | bytes 131088 | tf_op jit(solution)/shard_map/reduce_scatter | solution.py:134
  139.3 187.9 %all-to-all-done.1 = bf16[64,2,64,576]{3,2,1,0:T(8,128)(2,1)} async-done(((bf16[64,2,64,576]{3,2,1,0:T(8,128)(2,1)}), bf16[64,2,64,576]{3,2,1,0:T(8,128)(2,1)}, u32[]{:S(2)}, u32[]{:S(2)}) %all-to-all-start.1) | async-done | bytes 9437216 | tf_op jit(solution)/shard_map/all_to_all | solution.py:103
  327.2 7.5 %gather_fusion.3 = bf16[64,64,576]{2,1,0:T(8,128)(2,1)} fusion(bf16[128,64,576]{2,1,0:T(8,128)(2,1)} %bitcast.17, s32[1024]{0:T(1024)S(1)} %get-tuple-element.118), kind=kCustom, calls=%fused_computation.3 | custom fusion | bytes 9437440 | tf_op jit(solution)/shard_map/gather | solution.py:109
  334.7 7.6 %bitcast_select_fusion.1 = bf16[2,2048,576]{2,1,0:T(8,128)(2,1)} fusion(pred[2,2048]{1,0:T(4,128)(4,1)S(1)} %broadcast_in_dim.99, bf16[2,2048,576]{2,1,0:T(8,128)(2,1)} %bitcast.108, bf16[2,2048,576]{2,1,0:T(8,128)(2,1)} %bitcast.107), kind=kLoop, calls=%fused_computation.45 | loop fusion | flops 2359296 | bytes 14159872 | tf_op jit(solution)/shard_map/jit(_where)/select_n | solution.py:106
  342.3 7.8 %copy.35 = bf16[2,2048,576]{1,2,0:T(8,128)(2,1)} copy(bf16[2,2048,576]{2,1,0:T(8,128)(2,1)} %bitcast_select_fusion.1) | data formatting | bytes 9437184 | tf_op jit(solution)/shard_map/while | solution.py:122
  350.1 55.7 %while.20 = (s32[]{:T(128)}, bf16[2,64,2048]{2,1,0:T(8,128)(2,1)S(1)}, pred[2,64,2048]{2,1,0:T(8,128)(4,1)S(1)}, bf16[2,64,16,576]{3,2,1,0:T(8,128)(2,1)}, bf16[...) while((s32[]{:T(128)}, bf16[2,64,2048]{2,1,0:T(8,128)(2,1)S(1)}, ...), condition=%wide.region_7.8_spmd, body=%wide.region_4.7_spmd.sunk | while | flops 4717152256 | bytes 75637872 | solution.py:122
  350.1 8.7 %fusion.59 = f32[64,16,2048]{2,1,0:T(8,128)} fusion(bf16[2,2048,576]{1,2,0:T(8,128)(2,1)} %get-tuple-element.216, s32[]{:T(128)} %get-tuple-element.205, bf16[2,64,16,576]{3,2,1,0:T(8,128)(2,1)} %get-tuple-element.215), kind=kOutput, calls=%fused_computation.17.clone.1 | convolution fusion | flops 2415919104 | bytes 12059648 | tf_op jit(solution)/shard_map/while/body/eval_jaxpr/bhd,kd->bhk/dot_general | solution.py:43
  358.8 9.4 %fusion.60 = (f32[64,16]{1,0:T(8,128)S(1)}, f32[64,16,2048]{2,1,0:T(8,128)S(1)}) fusion(f32[64,16,2048]{2,1,0:T(8,128)} %fusion.59, pred[64,2048]{1,0:T(8,128)(4,1)S(1)} %dynamic-slice_bitcast_fusion.5), kind=kOutput, calls=%fused_computation.86.clone.1 | output fusion | flops 14682111 | bytes 16912384 | tf_op jit(solution)/shard_map/while/body/eval_jaxpr/sub | solution.py:48
  371.7 5.9 %fusion.61 = bf16[64,16,128]{2,0,1:T(8,128)(2,1)S(1)} fusion(bf16[16,512,128]{2,1,0:T(8,128)(2,1)} %get-tuple-element.217, bf16[2048,576]{0,1:T(8,128)(2,1)S(1)} %dynamic-slice_bitcast_fusion.4, bf16[64,16,2048]{2,1,0:T(8,128)(2,1)} %divide_convert_fusion.2), kind=kOutput, calls=%fused_computation.27.clone.1 | convolution fusion | flops 2282356736 | bytes 8650752 | tf_op jit(solution)/shard_map/while/body/eval_jaxpr/bhd,hde->bhe/dot_general | solution.py:53
  378.0 8.7 %fusion.59 = f32[64,16,2048]{2,1,0:T(8,128)} fusion(bf16[2,2048,576]{1,2,0:T(8,128)(2,1)} %get-tuple-element.216, s32[]{:T(128)} %get-tuple-element.205, bf16[2,64,16,576]{3,2,1,0:T(8,128)(2,1)} %get-tuple-element.215), kind=kOutput, calls=%fused_computation.17.clone.1 | convolution fusion | flops 2415919104 | bytes 12059648 | tf_op jit(solution)/shard_map/while/body/eval_jaxpr/bhd,kd->bhk/dot_general | solution.py:43
  386.7 9.4 %fusion.60 = (f32[64,16]{1,0:T(8,128)S(1)}, f32[64,16,2048]{2,1,0:T(8,128)S(1)}) fusion(f32[64,16,2048]{2,1,0:T(8,128)} %fusion.59, pred[64,2048]{1,0:T(8,128)(4,1)S(1)} %dynamic-slice_bitcast_fusion.5), kind=kOutput, calls=%fused_computation.86.clone.1 | output fusion | flops 14682111 | bytes 16912384 | tf_op jit(solution)/shard_map/while/body/eval_jaxpr/sub | solution.py:48
  399.6 5.8 %fusion.61 = bf16[64,16,128]{2,0,1:T(8,128)(2,1)S(1)} fusion(bf16[16,512,128]{2,1,0:T(8,128)(2,1)} %get-tuple-element.217, bf16[2048,576]{0,1:T(8,128)(2,1)S(1)} %dynamic-slice_bitcast_fusion.4, bf16[64,16,2048]{2,1,0:T(8,128)(2,1)} %divide_convert_fusion.2), kind=kOutput, calls=%fused_computation.27.clone.1 | convolution fusion | flops 2282356736 | bytes 8650752 | tf_op jit(solution)/shard_map/while/body/eval_jaxpr/bhd,hde->bhe/dot_general | solution.py:53
  (89 shorter events, 45.0 us)
Async XLA Ops:
  9.5 22.5 %all-to-all-start = ((s32[64,1,2]{2,1,0:T(1,128)}), s32[64,1,2]{2,1,0:T(1,128)S(1)}, u32[]{:S(2)}, u32[]{:S(2)}) async-start(s32[64,1,2]{2,1,0:T(1,128)} %copy.34), calls=%async_computation | async-start | bytes 65536 | tf_op jit(solution)/shard_map/all_to_all | solution.py:98
  34.5 55.2 %all-to-all-start.2 = ((bf16[64,2,64,128]{3,2,1,0:T(8,128)(2,1)}), bf16[64,2,64,128]{3,2,1,0:T(8,128)(2,1)}, u32[]{:S(2)}, u32[]{:S(2)}) async-start(bf16[64,2,64,128]{3,2,1,0:T(8,128)(2,1)} %bitcast.27), calls=%async_computation.2 | async-start | bytes 4194304 | tf_op jit(solution)/shard_map/all_to_all | solution.py:104
  40.1 6.6 %slice-start = ((f32[4096,5]{0,1:T(8,128)}), f32[4096,4]{0,1:T(4,128)S(1)}, s32[]{:S(2)}) async-start(f32[4096,5]{0,1:T(8,128)} %param.14), calls=%async_computation.5 | async-start | bytes 131072 | tf_op jit(solution)/shard_map/slice | solution.py:23
  65.5 6.0 %copy-start.1 = (bf16[4096,64]{1,0:T(8,128)(2,1)S(1)}, bf16[4096,64]{1,0:T(8,128)(2,1)}, u32[]{:S(2)}) copy-start(bf16[4096,64]{1,0:T(8,128)(2,1)} %copy.33) | copy-start | bytes 1572868
  89.7 8.1 %copy-start.6 = (s32[2,32]{1,0:T(2,128)S(1)}, s32[2,32]{1,0:T(2,128)}, u32[]{:S(2)}) copy-start(s32[2,32]{1,0:T(2,128)} %param.19) | copy-start | bytes 772
  89.7 10.8 %copy-start.3 = (bf16[128,2048]{1,0:T(8,128)(2,1)S(1)}, bf16[128,2048]{1,0:T(8,128)(2,1)}, u32[]{:S(2)}) copy-start(bf16[128,2048]{1,0:T(8,128)(2,1)} %param.16) | copy-start | bytes 1572868
  89.7 11.7 %copy-start.5 = (bf16[128,16]{0,1:T(8,128)(2,1)S(1)}, bf16[128,16]{0,1:T(8,128)(2,1)}, u32[]{:S(2)}) copy-start(bf16[128,16]{0,1:T(8,128)(2,1)} %param.17) | copy-start | bytes 12292
  89.7 237.5 %all-to-all-start.1 = ((bf16[64,2,64,576]{3,2,1,0:T(8,128)(2,1)}), bf16[64,2,64,576]{3,2,1,0:T(8,128)(2,1)}, u32[]{:S(2)}, u32[]{:S(2)}) async-start(bf16[64,2,64,576]{3,2,1,0:T(8,128)(2,1)} %bitcast.105), calls=%async_computation.1 | async-start | bytes 20971520 | tf_op jit(solution)/shard_map/all_to_all | solution.py:103
  97.5 40.2 %reduce-scatter.2.cloned.1.call-start = ((), (), s32[]{:S(2)}) async-start(), calls=%async_computation.4 | async-start | bytes 655360 | tf_op jit(solution)/shard_map/reduce_scatter | solution.py:134
  113.3 0.8 copy-start.4
  114.2 6.2 %copy-start.2 = (bf16[128,9216]{1,0:T(8,128)(2,1)S(1)}, bf16[128,9216]{1,0:T(8,128)(2,1)}, u32[]{:S(2)}) copy-start(bf16[128,9216]{1,0:T(8,128)(2,1)} %param.12) | copy-start | bytes 7077892
  342.3 7.8 %copy-start.7 = (bf16[2,64,2048]{2,1,0:T(8,128)(2,1)S(1)}, bf16[2,64,2048]{2,1,0:T(8,128)(2,1)}, u32[]{:S(2)}) copy-start(bf16[2,64,2048]{2,1,0:T(8,128)(2,1)} %custom-call.14) | copy-start | bytes 1572868
  368.2 3.2 copy-start
  396.1 3.2 copy-start
  405.8 0.8 copy-start.8
Sparse Core Ops, SparseCore 0:
  114.3 23.3 reduce-scatter.1
where the time goes:
time: 416 us; the launch traced here: 413 us
  waiting for transfers between devices  211 us (51%)
  local copies, waits for them, and re-layouts  74.1 us (18%)
  other arithmetic  51.1 us (12%)
  matrix products  35.9 us (9%)
  starting transfers between devices  26.8 us (6%)
  between operations  14.3 us (3%)
    all_to_all x1, waiting for transfers between devices, local(): lax.all_to_all(latent_blocks[asked_ids], 'ctx', split_axis=0, concat_axis...  188 us
    sub x2, other arithmetic, attend_block(): weights = jnp.where(visible[:, None, :], jnp.exp(masked - top_score), 0.0)  18.8 us
    dot_general x2, matrix products, attend_block(): jnp.einsum('bhd,kd->bhk', query_rows, picked, preferred_element_type=jnp....  17.4 us
    reduce_scatter x1, waiting for transfers between devices, local(): lax.psum_scatter(head_terms.reshape(-1, SEL * BLOCK).astype(jnp.bfloat16)...  13.9 us
    all_to_all x1, starting transfers between devices, local(): lax.all_to_all(requests, 'ctx', split_axis=0, concat_axis=0, tiled=True)  13.2 us
    dot_general x2, matrix products, attend_block(): jnp.einsum('bhd,hde->bhe', attended, value_up, preferred_element_type=jnp...  11.7 us
    gather x1, local copies, waits for them, and re-layouts, local(): latent_blocks[asked_ids]  10.2 us
    mul x1, local copies, waits for them, and re-layouts, dequantize(): latent_nope * cache_scales[:, :4, None]  9.43 us
  transfers between devices with their start and end apart: 4, of which 4 were waited for; matrix products, arithmetic and copies ran while one was open for 18% of the time, Pallas kernels for 0%

commit v1 on v0

v1 whole, which is shorter than its diff:
```python
from functools import partial

import jax
import jax.numpy as jnp
from jax import lax
from jax.experimental import pallas as pl
from jax.experimental.pallas import tpu as pltpu
from jax.sharding import PartitionSpec as P

D_LAT = 512
D_ROPE = 64
NOPE_DIM = 128
D_HEAD = 128
IDX_DIM = 128
BLOCK = 64
SEL = 32
D_KEY = 576
LANES = 128
MESH = pl.DeviceIdType.MESH
BF16 = jnp.bfloat16
F32 = jnp.float32
KEY_ROWS = IDX_DIM // 4
ROPE_ROWS = D_ROPE // 4
PARTS = (KEY_ROWS + ROPE_ROWS, 32, 32, 32, 32)
STEP = 4
APART = 8
VMEM_LIMIT = 60 * 1024 * 1024


def loop(low, high, step, unroll=None):
    def body(i, carry):
        step(i)
        return carry

    lax.fori_loop(low, high, body, 0, unroll=unroll)


def lanes_at(i):
    return pl.ds(pl.multiple_of(i * LANES, LANES), LANES)


def kernel(
    n,
    heads,
    sel_ref,
    w_ref,
    lat_hbm,
    keys_hbm,
    scales_hbm,
    q_hbm,
    iq_hbm,
    up_hbm,
    out_ref,
    logits_ref,
    latq,
    ropeq,
    keyq,
    scl,
    q,
    iq,
    up,
    reqs,
    req_in,
    req_rows,
    req_smem,
    picks_v,
    picks,
    lows,
    sends,
    recvs,
    lat,
    tail,
    key,
    wcol,
    terms,
    terms_in,
    qs,
    qr,
    load_sem,
    req_send,
    req_recv,
    send_sem,
    recv_sem,
    xsend,
    xrecv,
    isend,
    irecv,
    ready,
):
    me = lax.axis_index("ctx")
    hx = lax.axis_index("head")
    group = D_LAT // 4
    wide = SEL * BLOCK
    tiles = latq.shape[1] // LANES
    parts = range(len(PARTS))
    starts = [sum(PARTS[1:p]) for p in parts]

    loads = [
        pltpu.make_async_copy(keys_hbm, keyq, load_sem.at[0]),
        pltpu.make_async_copy(
            lat_hbm.at[pl.ds(D_LAT + hx * ROPE_ROWS, ROPE_ROWS), :], ropeq, load_sem.at[1]
        ),
        pltpu.make_async_copy(scales_hbm, scl, load_sem.at[2]),
        pltpu.make_async_copy(lat_hbm.at[pl.ds(hx * group, group), :], latq, load_sem.at[3]),
    ]
    later = [
        pltpu.make_async_copy(iq_hbm, iq, load_sem.at[4]),
        pltpu.make_async_copy(q_hbm, q, load_sem.at[5]),
        pltpu.make_async_copy(up_hbm, up, load_sem.at[6]),
    ]
    for copy in loads:
        copy.start()
    req_in[...] = jnp.zeros_like(req_in)

    barrier = pltpu.get_barrier_semaphore()

    def greet(j):
        pl.semaphore_signal(
            barrier, inc=1, device_id=(lax.rem(me + j, n), hx), device_id_type=MESH
        )

    loop(1, n, greet)
    for j in range(1, heads):
        pl.semaphore_signal(
            barrier, inc=1, device_id=(me, lax.rem(hx + j, heads)), device_id_type=MESH
        )

    chosen = jnp.concatenate([sel_ref[0:1, :], sel_ref[1:2, :]], axis=1)
    count = 2 * SEL
    kblocks = 2 * tiles
    owners = chosen // kblocks
    inside = chosen - owners * kblocks
    square = (count, count)
    across = jnp.broadcast_to(chosen, square)
    diagonal = lax.broadcasted_iota(jnp.int32, square, 0) == lax.broadcasted_iota(
        jnp.int32, square, 1
    )
    down = jnp.sum(jnp.where(diagonal, across, 0), axis=1, keepdims=True)
    smaller = (down // kblocks == across // kblocks) & (down < across)
    rank = jnp.max(smaller.astype(jnp.int32), axis=0, keepdims=True)
    odd = lax.broadcasted_iota(jnp.int32, (1, count), 1) % 2
    here = (owners == me).astype(jnp.int32)
    picks_v[...] = jnp.zeros_like(picks_v)
    picks_v[0:1, 0:count] = jnp.where(here > 0, 0, owners)
    picks_v[1:2, 0:count] = jnp.where(here > 0, inside + odd - 2 * odd * (inside % 2), 0)
    picks_v[2:3, 0:count] = here
    picks_v[3:4, 0:count] = (rank != odd).astype(jnp.int32)
    for k in range(n // 8):
        owner = lax.broadcasted_iota(jnp.int32, (8, count), 0) + 8 * k
        mine = jnp.broadcast_to(owners, (8, count)) == owner
        blocks = jnp.broadcast_to(inside, (8, count))
        one = jnp.min(jnp.where(mine, blocks, kblocks - 1), axis=1, keepdims=True)
        two = jnp.max(jnp.where(mine, blocks, 0), axis=1, keepdims=True)
        two = two + 1 - 2 * (two % 2)
        lane = lax.broadcasted_iota(jnp.int32, (8, LANES), 1)
        reqs[k] = jnp.where(lane == 0, one, two)
    picks_copy = pltpu.make_async_copy(picks_v, picks, load_sem.at[7])
    picks_copy.start()

    rows_at = lax.broadcasted_iota(jnp.int32, (KEY_ROWS, IDX_DIM), 0) + hx * KEY_ROWS
    cols_at = lax.broadcasted_iota(jnp.int32, (KEY_ROWS, IDX_DIM), 1)
    take = (rows_at == cols_at).astype(BF16)
    group_at = lax.broadcasted_iota(jnp.int32, (4, LANES), 0)

    def keep(p, t, block):
        lows[p][2 * t] = block.astype(BF16)
        lows[p][2 * t + 1] = pltpu.roll(block, BLOCK, 1).astype(BF16)

    def dequantize_first(t):
        at = lanes_at(t)
        part = lax.dot_general(
            take, keyq[at, :], (((1,), (1,)), ((), ())), preferred_element_type=F32
        )
        part = part * scl[4:5, at]
        keep(0, t, jnp.concatenate([part, ropeq[:, at].astype(F32)], axis=0))

    def dequantize_rest(t):
        at = lanes_at(t)
        mine = jnp.sum(jnp.where(group_at == hx, scl[0:4, at], 0.0), axis=0, keepdims=True)
        part = latq[:, at].astype(F32) * mine
        for p in parts[1:]:
            keep(p, t, part[starts[p] : starts[p] + PARTS[p]])

    for copy in loads[:3]:
        copy.wait()
    loop(0, tiles, dequantize_first, 4)

    pl.semaphore_wait(barrier, n + heads - 2)

    def request(o, c):
        return pltpu.make_async_remote_copy(
            src_ref=reqs.at[o // 8],
            dst_ref=req_in.at[c],
            send_sem=req_send.at[o],
            recv_sem=req_recv.at[c],
            device_id=(o, hx),
            device_id_type=MESH,
        )

    loop(0, me, lambda o: request(o, me).start())

    loads[3].wait()
    loop(0, tiles, dequantize_rest, 4)
    loop(me + 1, n, lambda c: request(me, c).wait_recv())
    row_at = lax.broadcasted_iota(jnp.int32, (n, 8, LANES), 1)
    req_rows[...] = jnp.sum(jnp.where(row_at == lax.rem(me, 8), req_in[...], 0), axis=1)
    to_smem = pltpu.make_async_copy(req_rows, req_smem, load_sem.at[8])
    to_smem.start()
    to_smem.wait()

    def block_copy(p, c, o):
        return pltpu.make_async_remote_copy(
            src_ref=sends[p].at[c],
            dst_ref=recvs[p].at[o],
            send_sem=send_sem.at[p, c],
            recv_sem=recv_sem.at[p, o],
            device_id=(c, hx),
            device_id_type=MESH,
        )

    def pack(p, c):
        one = req_smem[c, 0]
        two = req_smem[c, 1]
        sends[p][c, :, 0:BLOCK] = lows[p][one][:, 0:BLOCK]
        sends[p][c, :, BLOCK:LANES] = lows[p][two][:, BLOCK:LANES]

    def pack_first(c):
        pack(0, c)
        block_copy(0, c, me).start()

    loop(me + 1, n, pack_first)
    for copy in later:
        copy.start()
    picks_copy.wait()

    def send(p):
        def step(c):
            pack(p, c)
            block_copy(p, c, me).start()

        if p > 1:
            watched = (n - 1 - me) // APART

            @pl.when(watched > 0)
            def _():
                pl.semaphore_wait(ready.at[p - 2], watched)

            loop(me + 1, n, lambda c: block_copy(p - 2, c, me).wait_send())
        loop(me + 1, n, step)

    def outs(p):
        if p == 0:
            return (
                (key, KEY_ROWS, 0, lambda part: part * KEY_ROWS),
                (tail, ROPE_ROWS, KEY_ROWS, lambda part: part * ROPE_ROWS),
            )
        return ((lat, PARTS[p], 0, lambda part: part * group + starts[p]),)

    right, left, across_x = lax.rem(hx + 1, heads), lax.rem(hx + 3, heads), lax.rem(hx + 2, heads)
    to_right, to_left, on_right, on_left = range(4)

    def share(p, i, out, way, part, peer):
        ref, rows, _, place = out
        at = pl.ds(pl.multiple_of(place(part), ROPE_ROWS), rows)
        piece = ref.at[way - 2, at, :] if way >= 2 else ref.at[:, at, :]
        return pltpu.make_async_remote_copy(
            src_ref=piece,
            dst_ref=piece,
            send_sem=xsend.at[p + len(PARTS) * i, way],
            recv_sem=xrecv.at[p + len(PARTS) * i, way],
            device_id=(me, peer),
            device_id_type=MESH,
        )

    peers = [right, left, across_x]

    def receive(p):
        loop(0, me, lambda o: block_copy(p, o, o).wait_recv())
        if p < len(PARTS) - 2:
            loop(
                1,
                me // APART + 1,
                lambda k: pl.semaphore_signal(
                    ready.at[p], inc=1, device_id=(me - APART * k, hx), device_id_type=MESH
                ),
            )
        low_lanes = lax.broadcasted_iota(jnp.int32, (PARTS[p], LANES), 1) < BLOCK

        def choose(m):
            def entry(e):
                far = recvs[p][picks[0, e]].astype(F32)
                far = jnp.where(picks[3, e] > 0, pltpu.roll(far, BLOCK, 1), far)
                near = lows[p][picks[1, e]].astype(F32)
                return jnp.where(picks[2, e] > 0, near, far)

            tile = jnp.where(low_lanes, entry(2 * m), entry(2 * m + 1)).astype(BF16)
            row = m // (SEL // 2)
            for ref, rows, first, place in outs(p):
                at = pl.ds(pl.multiple_of(place(hx), ROPE_ROWS), rows)
                ref[row, at, lanes_at(lax.rem(m, SEL // 2))] = tile[first : first + rows]

        loop(0, SEL, choose, 4)
        for i, out in enumerate(outs(p)):
            share(p, i, out, to_right, hx, right).start()
            share(p, i, out, to_left, hx, left).start()

    def forward(p):
        for i, out in enumerate(outs(p)):
            share(p, i, out, to_right, left, hx).wait_recv()
            share(p, i, out, on_right, left, right).start()
            share(p, i, out, to_left, right, hx).wait_recv()
            share(p, i, out, on_left, right, left).start()

    def shared(p):
        for i, out in enumerate(outs(p)):
            share(p, i, out, on_right, across_x, hx).wait_recv()
            share(p, i, out, on_left, across_x, hx).wait_recv()

    send(1)

    column = lax.broadcasted_iota(jnp.int32, (BLOCK, wide), 1)
    token = lax.broadcasted_iota(jnp.int32, (BLOCK, wide), 0)
    for r in range(2):
        own = me * kblocks + kblocks - 2 + r
        at = lax.broadcasted_iota(jnp.int32, (1, SEL), 1)
        place = jnp.sum(jnp.where(sel_ref[r : r + 1, :] == own, at, 0), axis=1, keepdims=True)
        hidden = (column // BLOCK == place) & (column % BLOCK > token)
        tail[r, D_ROPE:, :] = jnp.where(hidden, -1e30, 0.0).astype(BF16)
    wcol[...] = jnp.transpose(w_ref[...].astype(F32)) * IDX_DIM**-0.5

    receive(0)
    send(2)
    receive(1)
    forward(0)
    send(3)
    receive(2)
    forward(1)
    send(4)
    shared(0)

    later[0].wait()
    idx_here = wcol.shape[1]

    def index_rows(r):
        rows = pl.ds(pl.multiple_of(r * BLOCK, BLOCK), BLOCK)
        weights = wcol[rows, :]
        total = jnp.zeros((BLOCK, wide), F32)
        for g in range(idx_here):
            dots = jnp.dot(
                iq[rows, g * IDX_DIM : (g + 1) * IDX_DIM], key[r], preferred_element_type=F32
            )
            total += weights[:, g : g + 1] * jnp.maximum(dots, 0.0)
        total = jnp.where(tail[r, D_ROPE:, :].astype(F32) < 0.0, 0.0, total).astype(BF16)
        share_wide = wide // heads
        for h in range(heads):
            terms[h, rows, :] = total[:, h * share_wide : (h + 1) * share_wide]

    loop(0, 2, index_rows)

    def term(part, peer):
        return pltpu.make_async_remote_copy(
            src_ref=terms.at[peer],
            dst_ref=terms_in.at[part],
            send_sem=isend.at[peer],
            recv_sem=irecv.at[part],
            device_id=(me, peer),
            device_id_type=MESH,
        )

    for peer in peers:
        term(hx, peer).start()

    later[1].wait()
    same = (
        lax.broadcasted_iota(jnp.int32, (BLOCK, BLOCK), 0)
        == lax.broadcasted_iota(jnp.int32, (BLOCK, BLOCK), 1)
    ).astype(BF16)
    groups = up.shape[0] // STEP

    def arrange(i):
        r, g = i // groups, lax.rem(i, groups)
        part = q[
            pl.ds(pl.multiple_of(r * BLOCK, BLOCK), BLOCK),
            pl.ds(pl.multiple_of(g * STEP * D_KEY, LANES), STEP * D_KEY),
        ]
        for h in range(STEP):
            rows = slice(h * BLOCK, (h + 1) * BLOCK)
            qs[i, rows, :] = part[:, h * D_KEY : h * D_KEY + D_LAT]
            qr[i, rows, :D_ROPE] = part[:, h * D_KEY + D_LAT : (h + 1) * D_KEY]
            qr[i, rows, D_ROPE:] = same

    loop(0, 2 * groups, arrange)
    receive(3)
    forward(2)
    for peer in peers:
        term(peer, hx).wait_recv()
    logits = terms[hx].astype(F32)
    for peer in peers:
        logits += terms_in[peer].astype(F32)
    logits_ref[...] = logits

    receive(4)
    forward(3)
    forward(4)
    for p in parts[3:]:
        loop(me + 1, n, lambda c, p=p: block_copy(p, c, me).wait_send())

    later[2].wait()
    for p in parts[1:]:
        shared(p)

    def attend(i):
        r, g = i // groups, lax.rem(i, groups)
        scores = jnp.dot(qs[i], lat[r], preferred_element_type=F32)
        scores += jnp.dot(qr[i], tail[r], preferred_element_type=F32)
        top = jnp.max(scores, axis=1, keepdims=True)
        scale = (NOPE_DIM + D_ROPE) ** -0.5 * 1.4426950408889634
        weights = jnp.exp2((scores - top) * scale)
        total = jnp.sum(weights, axis=1, keepdims=True)
        attended = lax.dot_general(
            weights.astype(BF16), lat[r], (((1,), (1,)), ((), ())), preferred_element_type=F32
        )
        attended = (attended / total).astype(BF16)
        rows = pl.ds(pl.multiple_of(r * BLOCK, BLOCK), BLOCK)
        for h in range(STEP):
            out = jnp.dot(
                attended[h * BLOCK : (h + 1) * BLOCK], up[g * STEP + h], preferred_element_type=F32
            )
            out_ref[rows, lanes_at(g * STEP + h)] = out.astype(BF16)

    loop(0, 2 * groups, attend)

    for p in parts:
        for i, out in enumerate(outs(p)):
            share(p, i, out, to_right, hx, right).wait_send()
            share(p, i, out, to_left, hx, left).wait_send()
            share(p, i, out, on_right, left, right).wait_send()
            share(p, i, out, on_left, right, left).wait_send()
    for peer in peers:
        term(hx, peer).wait_send()
    loop(0, me, lambda o: request(o, me).wait_send())


def local(
    queries,
    cache_latent,
    cache_scales,
    index_keys,
    index_queries,
    index_weights,
    value_up,
    selections,
):
    n = lax.axis_size("ctx")
    heads = lax.axis_size("head")
    tokens = index_keys.shape[0]
    qtokens = queries.shape[0]
    kblocks = tokens // BLOCK
    heads_here = value_up.shape[0]
    idx_here = index_weights.shape[1]
    wide = SEL * BLOCK
    any_spec = pl.BlockSpec(memory_space=pl.ANY)
    vmem_spec = pl.BlockSpec(memory_space=pltpu.VMEM)
    dma = pltpu.SemaphoreType.DMA
    vmem = pltpu.VMEM
    steps = 2 * heads_here // STEP
    return pl.pallas_call(
        partial(kernel, n, heads),
        out_shape=(
            jax.ShapeDtypeStruct((qtokens, heads_here * D_HEAD), BF16),
            jax.ShapeDtypeStruct((qtokens, wide // heads), F32),
        ),
        in_specs=[vmem_spec] * 2 + [any_spec] * 6,
        out_specs=(vmem_spec,) * 2,
        scratch_shapes=[
            vmem((D_LAT // 4, tokens), BF16),
            vmem((ROPE_ROWS, tokens), BF16),
            vmem((tokens, IDX_DIM), BF16),
            vmem((5, tokens), F32),
            vmem(queries.shape, BF16),
            vmem(index_queries.shape, BF16),
            vmem(value_up.shape, BF16),
            vmem((n // 8, 8, LANES), jnp.int32),
            vmem((n, 8, LANES), jnp.int32),
            vmem((n, LANES), jnp.int32),
            pltpu.SMEM((n, LANES), jnp.int32),
            vmem((8, LANES), jnp.int32),
            pltpu.SMEM((8, LANES), jnp.int32),
            [vmem((kblocks, rows, LANES), BF16) for rows in PARTS],
            [vmem((n, rows, LANES), BF16) for rows in PARTS],
            [vmem((n, rows, LANES), BF16) for rows in PARTS],
            vmem((2, D_LAT, wide), BF16),
            vmem((2, D_ROPE + BLOCK, wide), BF16),
            vmem((2, IDX_DIM, wide), BF16),
            vmem((qtokens, idx_here), F32),
            vmem((heads, qtokens, wide // heads), BF16),
            vmem((heads, qtokens, wide // heads), BF16),
            vmem((steps, STEP * BLOCK, D_LAT), BF16),
            vmem((steps, STEP * BLOCK, 2 * D_ROPE), BF16),
            dma((9,)),
            dma((n,)),
            dma((n,)),
            dma((len(PARTS), n)),
            dma((len(PARTS), n)),
            dma((len(PARTS) + 1, heads)),
            dma((len(PARTS) + 1, heads)),
            dma((heads,)),
            dma((heads,)),
            pltpu.SemaphoreType.REGULAR((len(PARTS),)),
        ],
        compiler_params=pltpu.CompilerParams(
            collective_id=0, has_side_effects=True, vmem_limit_bytes=VMEM_LIMIT
        ),
        name="sparse_attention",
    )(
        selections,
        index_weights.T,
        cache_latent.T,
        index_keys,
        cache_scales.T,
        queries,
        index_queries,
        value_up,
    )


def solution(mesh):
    return jax.shard_map(
        local,
        mesh=mesh,
        in_specs=(
            P("ctx", "head"),
            P("ctx", None),
            P("ctx", None),
            P("ctx", None),
            P("ctx", "head"),
            P("ctx", "head"),
            P("head", None, None),
            P("ctx", None),
        ),
        out_specs=(P("ctx", "head"), P("ctx", "head")),
        check_vma=False,
    )
```

time: 416 us -> 137 us (0.33)
  waiting for transfers between devices: 211 us -> 0 us
  Pallas kernels: 0 us -> 133 us
  local copies, waits for them, and re-layouts: 74.1 us -> 3.55 us
  other arithmetic: 51.1 us -> 0 us
  matrix products: 35.9 us -> 0 us
  starting transfers between devices: 26.8 us -> 0 us
  between operations: 14.3 us -> 0.64 us
    all_to_all x3 -> x0, waiting for transfers between devices: 197 us -> none  [the longest x1 188 us: local(): lax.all_to_all(latent_blocks[asked_ids], 'ctx', split_axis=0, concat_axis...]
    pallas_call x0 -> x1, Pallas kernels: none -> 133 us  [local(): pl.pallas_call(partial(kernel, n, heads), out_shape=(jax.ShapeDtypeStruct...]
    dot_general x6 -> x0, matrix products: 35.9 us -> none  [the longest x2 17.4 us: attend_block(): jnp.einsum('bhd,kd->bhk', query_rows, picked, preferred_element_type=jnp....]
    gather x7 -> x0, local copies, waits for them, and re-layouts: 30 us -> none  [the longest x1 10.2 us: local(): latent_blocks[asked_ids]]
    all_to_all x3 -> x0, starting transfers between devices: 26.5 us -> none  [the longest x1 13.2 us: local(): lax.all_to_all(requests, 'ctx', split_axis=0, concat_axis=0, tiled=True)]
    sub x3 -> x0, other arithmetic: 18.8 us -> none  [the longest x2 18.8 us: attend_block(): weights = jnp.where(visible[:, None, :], jnp.exp(masked - top_score), 0.0)]
    reduce_scatter x1 -> x0, waiting for transfers between devices: 13.9 us -> none  [local(): lax.psum_scatter(head_terms.reshape(-1, SEL * BLOCK).astype(jnp.bfloat16)...]
    slice x7 -> x0, local copies, waits for them, and re-layouts: 10.5 us -> none  [the longest x1 4.68 us: dequantize(): cache_latent[:, :D_LAT].astype(jnp.float32)]
  transfers between devices with their start and end apart: 4 -> 0, of which waited for: 4 -> 0; matrix products, arithmetic and copies ran while one was open for 18% -> 0% of each run, Pallas kernels for 0% -> 0%
where the time goes in v1:
time: 137 us
  Pallas kernels  133 us (97%)
  local copies, waits for them, and re-layouts  3.55 us (3%)
    pallas_call x1, Pallas kernels, local(): pl.pallas_call(partial(kernel, n, heads), out_shape=(jax.ShapeDtypeStruct...  133 us
    unnamed x2, local copies, waits for them, and re-layouts  3.55 us

profile of v1, /device:TPU:1, one launch (start us, length us, event | category | flops | bytes accessed | tf_op | source)
XLA Modules:
  0.0 137.0 jit_solution(1755753126312093302)
XLA Ops:
  0.6 132.8 %sparse_attention.1 = (bf16[128,2048]{1,0:T(8,128)(2,1)}, f32[128,512]{1,0:T(8,128)}) custom-call(s32[2,32]{1,0:T(2,128)} %sel_ref.1, bf16[16,128]{1,0:T(8,128)(2,1)} %bitcast.5, bf16[576,4096]{1,0:T(8,128)(2,1)} %bitcast.3, bf16[4096,128]{1,0:T(8,128)(2,1)} %keys_hbm.1, f32[5,4096]{1,0:T(8,128)} %bitcast.4, bf16[128,9216]{1,0:T(8,128)(2,1)} %q_hbm.1, ...), custom_call_target="tpu_custom_call" | custom-call | tf_op jit(solution)/shard_map/sparse_attention/pallas_call | solution.py:467
  133.4 1.9 %copy.12 = bf16[128,2048]{1,0:T(8,128)(2,1)} copy(bf16[128,2048]{1,0:T(8,128)(2,1)} %get-tuple-element.4) | data formatting | bytes 1048576
  135.3 1.7 %copy.13 = f32[128,512]{1,0:T(8,128)} copy(f32[128,512]{1,0:T(8,128)} %get-tuple-element.5) | data formatting | bytes 524288

commit v2 on v1

--- a/solution.py
+++ b/solution.py
@@ -22,7 +22,7 @@
 KEY_ROWS = IDX_DIM // 4
 ROPE_ROWS = D_ROPE // 4
 PARTS = (KEY_ROWS + ROPE_ROWS, 32, 32, 32, 32)
-STEP = 4
+STEP = 8
 APART = 8
 VMEM_LIMIT = 60 * 1024 * 1024
 

time: 137 us -> 135 us (0.985)
  Pallas kernels: 133 us -> 131 us
    pallas_call x1, Pallas kernels: 133 us -> 131 us  [local(): pl.pallas_call(partial(kernel, n, heads), out_shape=(jax.ShapeDtypeStruct...]
where the time goes in v2:
time: 135 us
  Pallas kernels  131 us (97%)
  local copies, waits for them, and re-layouts  3.55 us (3%)
    pallas_call x1, Pallas kernels, local(): pl.pallas_call(partial(kernel, n, heads), out_shape=(jax.ShapeDtypeStruct...  131 us
    unnamed x2, local copies, waits for them, and re-layouts  3.55 us

profile of v2, /device:TPU:1, one launch (start us, length us, event | category | flops | bytes accessed | tf_op | source)
XLA Modules:
  0.0 135.1 jit_solution(8853326991080839457)
XLA Ops:
  0.6 130.9 %sparse_attention.1 = (bf16[128,2048]{1,0:T(8,128)(2,1)}, f32[128,512]{1,0:T(8,128)}) custom-call(s32[2,32]{1,0:T(2,128)} %sel_ref.1, bf16[16,128]{1,0:T(8,128)(2,1)} %bitcast.5, bf16[576,4096]{1,0:T(8,128)(2,1)} %bitcast.3, bf16[4096,128]{1,0:T(8,128)(2,1)} %keys_hbm.1, f32[5,4096]{1,0:T(8,128)} %bitcast.4, bf16[128,9216]{1,0:T(8,128)(2,1)} %q_hbm.1, ...), custom_call_target="tpu_custom_call" | custom-call | tf_op jit(solution)/shard_map/sparse_attention/pallas_call | solution.py:467
  131.6 1.9 %copy.12 = bf16[128,2048]{1,0:T(8,128)(2,1)} copy(bf16[128,2048]{1,0:T(8,128)(2,1)} %get-tuple-element.4) | data formatting | bytes 1048576
  133.5 1.7 %copy.13 = f32[128,512]{1,0:T(8,128)} copy(f32[128,512]{1,0:T(8,128)} %get-tuple-element.5) | data formatting | bytes 524288

commit v3 on v2

--- a/solution.py
+++ b/solution.py
@@ -22,7 +22,7 @@
 KEY_ROWS = IDX_DIM // 4
 ROPE_ROWS = D_ROPE // 4
 PARTS = (KEY_ROWS + ROPE_ROWS, 32, 32, 32, 32)
-STEP = 8
+STEP = 16
 APART = 8
 VMEM_LIMIT = 60 * 1024 * 1024
 

time: 135 us -> 135 us (level)
  no operation moved by 1% of the time
where the time goes in v3:
time: 135 us
  Pallas kernels  131 us (97%)
  local copies, waits for them, and re-layouts  3.55 us (3%)
    pallas_call x1, Pallas kernels, local(): pl.pallas_call(partial(kernel, n, heads), out_shape=(jax.ShapeDtypeStruct...  131 us
    unnamed x2, local copies, waits for them, and re-layouts  3.55 us

profile of v3, /device:TPU:1, one launch (start us, length us, event | category | flops | bytes accessed | tf_op | source)
XLA Modules:
  0.0 134.9 jit_solution(10521305367372135105)
XLA Ops:
  0.6 130.7 %sparse_attention.1 = (bf16[128,2048]{1,0:T(8,128)(2,1)}, f32[128,512]{1,0:T(8,128)}) custom-call(s32[2,32]{1,0:T(2,128)} %sel_ref.1, bf16[16,128]{1,0:T(8,128)(2,1)} %bitcast.5, bf16[576,4096]{1,0:T(8,128)(2,1)} %bitcast.3, bf16[4096,128]{1,0:T(8,128)(2,1)} %keys_hbm.1, f32[5,4096]{1,0:T(8,128)} %bitcast.4, bf16[128,9216]{1,0:T(8,128)(2,1)} %q_hbm.1, ...), custom_call_target="tpu_custom_call" | custom-call | tf_op jit(solution)/shard_map/sparse_attention/pallas_call | solution.py:467
  131.4 1.9 %copy.12 = bf16[128,2048]{1,0:T(8,128)(2,1)} copy(bf16[128,2048]{1,0:T(8,128)(2,1)} %get-tuple-element.4) | data formatting | bytes 1048576
  133.2 1.7 %copy.13 = f32[128,512]{1,0:T(8,128)} copy(f32[128,512]{1,0:T(8,128)} %get-tuple-element.5) | data formatting | bytes 524288

commit v4 on v3

--- a/solution.py
+++ b/solution.py
@@ -228,7 +228,9 @@
         pack(0, c)
         block_copy(0, c, me).start()
 
-    loop(me + 1, n, pack_first)
+    halfway = me + 1 + (n - 1 - me) // 2
+    loop(halfway, n, pack_first)
+    loop(me + 1, halfway, pack_first)
     for copy in later:
         copy.start()
     picks_copy.wait()
@@ -246,7 +248,8 @@
                 pl.semaphore_wait(ready.at[p - 2], watched)
 
             loop(me + 1, n, lambda c: block_copy(p - 2, c, me).wait_send())
-        loop(me + 1, n, step)
+        loop(halfway, n, step)
+        loop(me + 1, halfway, step)
 
     def outs(p):
         if p == 0:

time: 135 us -> 134 us (level)
  Pallas kernels: 131 us -> 129 us
    pallas_call x1, Pallas kernels: 131 us -> 129 us  [local(): pl.pallas_call(partial(kernel, n, heads), out_shape=(jax.ShapeDtypeStruct...]
where the time goes in v4:
time: 134 us; the launch traced here: 133 us
  Pallas kernels  129 us (96%)
  local copies, waits for them, and re-layouts  3.55 us (3%)
    pallas_call x1, Pallas kernels, local(): pl.pallas_call(partial(kernel, n, heads), out_shape=(jax.ShapeDtypeStruct...  129 us
    unnamed x2, local copies, waits for them, and re-layouts  3.55 us

profile of v4, /device:TPU:1, one launch (start us, length us, event | category | flops | bytes accessed | tf_op | source)
XLA Modules:
  0.0 133.4 jit_solution(10466033826547012526)
XLA Ops:
  0.6 129.2 %sparse_attention.1 = (bf16[128,2048]{1,0:T(8,128)(2,1)}, f32[128,512]{1,0:T(8,128)}) custom-call(s32[2,32]{1,0:T(2,128)} %sel_ref.1, bf16[16,128]{1,0:T(8,128)(2,1)} %bitcast.5, bf16[576,4096]{1,0:T(8,128)(2,1)} %bitcast.3, bf16[4096,128]{1,0:T(8,128)(2,1)} %keys_hbm.1, f32[5,4096]{1,0:T(8,128)} %bitcast.4, bf16[128,9216]{1,0:T(8,128)(2,1)} %q_hbm.1, ...), custom_call_target="tpu_custom_call" | custom-call | tf_op jit(solution)/shard_map/sparse_attention/pallas_call | solution.py:470
  129.9 1.9 %copy.12 = bf16[128,2048]{1,0:T(8,128)(2,1)} copy(bf16[128,2048]{1,0:T(8,128)(2,1)} %get-tuple-element.4) | data formatting | bytes 1048576
  131.8 1.7 %copy.13 = f32[128,512]{1,0:T(8,128)} copy(f32[128,512]{1,0:T(8,128)} %get-tuple-element.5) | data formatting | bytes 524288
